TPU v7x, 32 devices: a whole 2x2x4 slice. The times are simulated.
32 devices in a mesh: groups: 2 (over y), dp: 8 (over z, x), section: 2 (over core).
Axes of the slice: x: 2, y: 2, z: 4, core: 2. Of those that a mesh axis runs over, the one named last changes fastest.
Arguments:
- latents: bfloat16 [2048, 3072], P(('groups', 'dp')), parts along dimension 0, may hold values from -6 to 6
- out_grad: float32 [2048, 3072], P(('groups', 'dp')), parts along dimension 0, may hold values from -0.3 to 0.3
- frozen_weight: bfloat16 [2, 3072, 1536], P('section', 'dp'), may hold values from -0.109375 to 0.109375
- norm_gain: float32 [2, 3072], P('section'), may hold values from 0.5 to 1.5
- time_gate: float32 [2, 50], P('section'), may hold values from 0.5 to 2
- down_factors: bfloat16 [2, 96, 64, 3072], P('section', ('groups', 'dp')), parts along dimension 1, may hold values from -0.109375 to 0.109375
- up_factors: bfloat16 [2, 96, 64, 1536], P('section', ('groups', 'dp')), parts along dimension 1, may hold values from -0.75 to 0.75
- block_jobs: int32 [16], P('groups'), parts along dimension 0, may hold values from 0 to 47
- owners: int32 [96], P('groups'), parts along dimension 0, may hold values from 0 to 47, as said below
- block_steps: int32 [16], P(('groups', 'dp')), parts along dimension 0, may hold values from 0 to 49
- block_fill: int32 [16], P(('groups', 'dp')), parts along dimension 0, may hold values from 1 to 128, as said below
Outputs:
- grad_down: float32 [2, 96, 64, 3072], P('section', ('groups', 'dp')), parts along dimension 1
- grad_up: float32 [2, 96, 64, 1536], P('section', ('groups', 'dp')), parts along dimension 1
There are 2 independent parts, one for each index of `groups`. A program takes and returns all parts, laid end to end along the dimension named above; an argument that names none is the same for every part. Nothing has to cross between parts.
Inputs may be any that keep to these rules, and one draw needn't show every extreme that they name: `owners`: no two adapters share a slot; slot 0 and the last slot always hold one. `block_fill`: the live rows come first in their block; in every draw some block is full and some holds a single live row.
All inputs are finite; a program needn't handle non-finite values.
Results may differ from a plain program's by a relative error of at most 0.006.
Values may be sent and summed in bfloat16 or wider, within the bound.
A program may use at most 128 MiB of HBM per device.

v0:
```python
import jax
import jax.numpy as jnp
from jax import lax
from jax.sharding import PartitionSpec as P

epsilon = 1e-06


def passed_along(value, axis, steps):
    count = lax.axis_size(axis)
    leading, last = (max(0, -steps), min(count, count - steps))
    return lax.ppermute(value, axis, [(source, source + steps) for source in range(leading, last)])


def matrix_product(spec, left_op, right_op):
    return jnp.einsum(spec, left_op, right_op, preferred_element_type=jnp.float32)


def forward_pass(inputs, frozen_layer, gain_row, down_projection_block, up_block, scales):
    out_width = up_block.shape[2]
    block_total, row_count, model_width = inputs.shape
    values = inputs.astype(jnp.float32)
    inverse = lax.rsqrt(jnp.mean(values * values, axis=2) + epsilon)
    normalized_input = (values * inverse[:, :, None] * gain_row).astype(jnp.bfloat16)
    frozen_out = jnp.dot(
        normalized_input.reshape(block_total * row_count, model_width),
        frozen_layer,
        preferred_element_type=jnp.float32,
    )
    frozen_out = frozen_out.reshape(block_total, row_count, out_width)
    reduced_features = matrix_product(
        "uyi,uoi->uyo", normalized_input, down_projection_block
    ).astype(jnp.bfloat16)
    extra = matrix_product("bmq,bqh->bmh", reduced_features, up_block)
    update = scales[:, None, None] * (frozen_out + extra)
    window_out = (values[:, :, :out_width] + update).astype(jnp.bfloat16)
    outputs = jnp.concatenate([window_out, inputs[:, :, out_width:]], axis=2)
    return (outputs, (inputs, normalized_input, inverse, reduced_features))


def backward_pass(
    stored, cotangent, frozen_layer, gain_row, down_projection_block, up_block, scales
):
    inputs, normalized_input, inverse, reduced_features = stored
    out_width = up_block.shape[2]
    block_total, row_count, model_width = inputs.shape
    values = inputs.astype(jnp.float32)
    delta_output = (scales[:, None, None] * cotangent[:, :, :out_width]).astype(jnp.bfloat16)
    grad_upper = matrix_product("bmq,bmh->bqh", reduced_features, delta_output)
    low_rank_delta = matrix_product("bmh,bqh->bmq", delta_output, up_block).astype(jnp.bfloat16)
    lower_gradient = matrix_product("hoc,hou->hcu", low_rank_delta, normalized_input)
    through = lax.dot_general(
        delta_output.reshape(block_total * row_count, out_width),
        frozen_layer,
        (((1,), (1,)), ((), ())),
        preferred_element_type=jnp.float32,
    )
    delta_normalized = through.reshape(block_total, row_count, model_width) + matrix_product(
        "rha,rak->rhk", low_rank_delta, down_projection_block
    )
    scaled = gain_row * delta_normalized
    inner = jnp.mean(values * scaled, axis=2)
    cubed = inverse * inverse * inverse
    delta_in = inverse[:, :, None] * scaled - values * (cubed * inner)[:, :, None]
    carried = (cotangent + delta_in).astype(jnp.bfloat16)
    return (carried, lower_gradient, grad_upper)


def body(
    latents,
    out_grad,
    frozen_weight,
    norm_gain,
    time_gate,
    down_factors,
    up_factors,
    block_jobs,
    owners,
    block_steps,
    block_fill,
):
    position = lax.axis_index("section")
    lane_count = lax.axis_size("dp")
    slot_local = down_factors.shape[1]
    low_rank = down_factors.shape[2]
    model_width = down_factors.shape[3]
    blocks_dev = block_fill.shape[0]
    block_rows = latents.shape[0] // blocks_dev
    is_first = position == 0
    frozen_layer = lax.all_gather(frozen_weight[0], "dp", axis=0, tiled=True)
    gain_row = norm_gain[0]
    gate_row = time_gate[0]
    chosen = block_steps[:, None] == jnp.arange(gate_row.shape[0], dtype=jnp.int32)[None, :]
    scales = jnp.sum(jnp.where(chosen, gate_row[None, :], 0.0), axis=1)
    matches = block_jobs[:, None] == jnp.arange(owners.shape[0], dtype=jnp.int32)[None, :]
    slot_of = jnp.sum(jnp.where(matches, owners[None, :], 0), axis=1)
    spread_down, spread_up = (
        lax.all_to_all(down_factors[0], "dp", split_axis=2, concat_axis=0, tiled=True),
        lax.all_to_all(up_factors[0], "dp", split_axis=2, concat_axis=0, tiled=True),
    )
    down_projection_block, up_block = (
        lax.all_to_all(spread_down[slot_of], "dp", split_axis=0, concat_axis=2, tiled=True),
        lax.all_to_all(spread_up[slot_of], "dp", split_axis=0, concat_axis=2, tiled=True),
    )
    micro_count = 1
    micro_rows = block_rows // micro_count
    block_view = latents.reshape(blocks_dev, block_rows, model_width)
    live_rows = jnp.arange(block_rows, dtype=jnp.int32)[None, :] < block_fill[:, None]
    masked = jnp.where(
        live_rows[:, :, None], out_grad.reshape(blocks_dev, block_rows, model_width), 0.0
    )
    incoming = jnp.zeros((blocks_dev, micro_rows, model_width), jnp.bfloat16)
    kept = []
    for turn_index in range(micro_count + 1):
        source = jnp.where(is_first, block_view, incoming)
        outputs, stored = forward_pass(
            source, frozen_layer, gain_row, down_projection_block, up_block, scales
        )
        kept.append(stored)
        if turn_index < micro_count:
            incoming = passed_along(outputs, "section", 1)
    states = [
        jax.tree.map(lambda former, latter: jnp.where(is_first, former, latter), kept[0], kept[1])
    ]
    returned = jnp.zeros((blocks_dev, micro_rows, model_width), jnp.bfloat16)
    sum_down = jnp.zeros((blocks_dev, low_rank, model_width), jnp.float32)
    sum_up = jnp.zeros((blocks_dev, low_rank, up_block.shape[2]), jnp.float32)
    for turn_index in range(micro_count + 1):
        late_micro = min(turn_index, micro_count - 1)
        early_micro = max(turn_index - 1, 0)
        current = jax.tree.map(
            lambda former, latter: jnp.where(is_first, former, latter),
            states[early_micro],
            states[late_micro],
        )
        cotangent = jnp.where(is_first, returned.astype(jnp.float32), masked)
        carried, lower_gradient, grad_upper = backward_pass(
            current, cotangent, frozen_layer, gain_row, down_projection_block, up_block, scales
        )
        useful = jnp.where(is_first, turn_index >= 1, turn_index < micro_count)
        sum_down = sum_down + jnp.where(useful, lower_gradient, 0.0)
        sum_up = sum_up + jnp.where(useful, grad_upper, 0.0)
        if turn_index < micro_count:
            returned = passed_along(carried, "section", -1)
    pieces_down, pieces_up = (
        lax.all_to_all(sum_down, "dp", split_axis=2, concat_axis=0, tiled=True),
        lax.all_to_all(sum_up, "dp", split_axis=2, concat_axis=0, tiled=True),
    )
    slot_total = lane_count * slot_local
    onehot = (jnp.arange(slot_total, dtype=jnp.int32)[:, None] == slot_of[None, :]).astype(
        jnp.float32
    )
    block_total = pieces_down.shape[0]
    slot_down = jnp.dot(
        onehot,
        pieces_down.reshape(block_total, -1),
        precision=lax.Precision.HIGHEST,
        preferred_element_type=jnp.float32,
    )
    slot_up = jnp.dot(
        onehot,
        pieces_up.reshape(block_total, -1),
        precision=lax.Precision.HIGHEST,
        preferred_element_type=jnp.float32,
    )
    slot_down = slot_down.reshape(slot_total, low_rank, pieces_down.shape[2])
    slot_up = slot_up.reshape(slot_total, low_rank, pieces_up.shape[2])
    owned_down, owned_up = (
        lax.all_to_all(slot_down, "dp", split_axis=0, concat_axis=2, tiled=True),
        lax.all_to_all(slot_up, "dp", split_axis=0, concat_axis=2, tiled=True),
    )
    return (owned_down[None], owned_up[None])


def solution(mesh):
    placed = (
        P(("groups", "dp"), None),
        P(("groups", "dp"), None),
        P("section", "dp", None),
        P("section", None),
        P("section", None),
        P("section", ("groups", "dp"), None, None),
        P("section", ("groups", "dp"), None, None),
        P("groups"),
        P("groups"),
        P(("groups", "dp")),
        P(("groups", "dp")),
    )
    return jax.shard_map(
        body,
        mesh=mesh,
        in_specs=placed,
        out_specs=(
            P("section", ("groups", "dp"), None, None),
            P("section", ("groups", "dp"), None, None),
        ),
        check_vma=False,
    )
```

profile of v0, /device:TPU:0, one launch (start us, length us, event | category | flops | bytes accessed | tf_op | source)
XLA Modules:
  0.0 536.9 jit_solution(2931471331591064361)
XLA Ops:
  17.0 7.4 %all-to-all-start = ((bf16[8,2,36864]{2,1,0:T(2,128)(2,1)}), bf16[8,2,36864]{2,1,0:T(2,128)(2,1)S(1)}, u32[]{:S(2)}, u32[]{:S(2)}) async-start(bf16[8,2,36864]{2,1,0:T(2,128)(2,1)} %reshape.236), calls=%async_computation | async-start | bytes 2359296 | tf_op jit(solution)/shard_map/all_to_all | solution.py:99
  24.4 6.0 %copy.68 = bf16[1,6,64,3072]{2,1,3,0:T(8,128)(2,1)} copy(bf16[1,6,64,3072]{3,2,1,0:T(8,128)(2,1)S(1)} %copy-done.7) | data formatting | bytes 4718592 | tf_op args[5]
  30.4 6.4 %bitcast_bitcast_fusion = bf16[3072,6,64]{2,1,0:T(8,128)(2,1)} fusion(bf16[1,6,64,3072]{2,1,3,0:T(8,128)(2,1)} %copy.68), kind=kLoop, calls=%fused_computation.81 | loop fusion | bytes 4718592
  36.8 8.5 %reshape.238 = bf16[8,2,73728]{2,1,0:T(2,128)(2,1)} reshape(bf16[3072,6,64]{2,1,0:T(8,128)(2,1)} %bitcast_bitcast_fusion) | data formatting | bytes 4718592
  45.3 38.7 %all-to-all-done = bf16[8,2,36864]{2,1,0:T(2,128)(2,1)S(1)} async-done(((bf16[8,2,36864]{2,1,0:T(2,128)(2,1)}), bf16[8,2,36864]{2,1,0:T(2,128)(2,1)S(1)}, u32[]{:S(2)}, u32[]{:S(2)}) %all-to-all-start) | async-done | bytes 1179680 | tf_op jit(solution)/shard_map/all_to_all | solution.py:99
  85.0 4.4 all-to-all-start.2
  101.9 98.6 %all-to-all-done.2 = bf16[8,2,73728]{2,1,0:T(2,128)(2,1)} async-done(((bf16[8,2,73728]{2,1,0:T(2,128)(2,1)}), bf16[8,2,73728]{2,1,0:T(2,128)(2,1)}, u32[]{:S(2)}, u32[]{:S(2)}) %all-to-all-start.2) | async-done | bytes 2359328 | tf_op jit(solution)/shard_map/all_to_all | solution.py:98
  200.6 9.3 %all-to-all-start.1 = ((bf16[8,64,192]{2,1,0:T(8,128)(2,1)}), bf16[8,64,192]{2,1,0:T(8,128)(2,1)S(1)}, u32[]{:S(2)}, u32[]{:S(2)}) async-start(bf16[8,64,192]{2,1,0:T(8,128)(2,1)} %gather_fusion), calls=%async_computation.1 | async-start | bytes 524288 | tf_op jit(solution)/shard_map/all_to_all | solution.py:103
  213.5 8.2 %reshape.239 = bf16[3072,6,64]{2,1,0:T(8,128)(2,1)} reshape(bf16[8,2,73728]{2,1,0:T(2,128)(2,1)} %all-to-all-done.2) | data formatting | bytes 4718592
  221.7 6.7 %copy.70 = bf16[8,6,64,384]{3,2,1,0:T(8,128)(2,1)} copy(bf16[8,6,64,384]{2,1,3,0:T(8,128)(2,1)} %bitcast.151) | data formatting | bytes 4718592 | tf_op jit(solution)/shard_map/all_to_all | solution.py:98
  231.5 6.0 %all-to-all-start.3 = ((bf16[8,64,384]{2,1,0:T(8,128)(2,1)}), bf16[8,64,384]{2,1,0:T(8,128)(2,1)S(1)}, u32[]{:S(2)}, u32[]{:S(2)}) async-start(bf16[8,64,384]{2,1,0:T(8,128)(2,1)} %gather_fusion.1), calls=%async_computation.3 | async-start | bytes 786432 | tf_op jit(solution)/shard_map/all_to_all | solution.py:102
  241.2 7.4 %all-to-all-done.3 = bf16[8,64,384]{2,1,0:T(8,128)(2,1)S(1)} async-done(((bf16[8,64,384]{2,1,0:T(8,128)(2,1)}), bf16[8,64,384]{2,1,0:T(8,128)(2,1)S(1)}, u32[]{:S(2)}, u32[]{:S(2)}) %all-to-all-start.3) | async-done | bytes 393248 | tf_op jit(solution)/shard_map/all_to_all | solution.py:102
  250.0 5.3 fusion.2
  272.8 7.1 %reduce.7 = f32[1536,64]{1,0:T(8,128)S(1)} reduce(f32[1536,1,64]{2,1,0:T(1,128)S(1)} %bitcast.157, f32[]{:T(128)} %broadcast.202), dimensions={1}, to_apply=%bitcast.124.reduce_sub_computation | reduce | bytes 786436
  290.5 13.6 %reduce.5 = f32[3072,64]{1,0:T(8,128)S(1)} reduce(f32[3072,1,64]{2,1,0:T(1,128)S(1)} %bitcast.155, f32[]{:T(128)} %broadcast.202), dimensions={1}, to_apply=%bitcast.122.reduce_sub_computation | reduce | bytes 1572868
  305.9 6.3 %all-to-all-start.4 = ((f32[8,1,24576]{2,1,0:T(1,128)}), f32[8,1,24576]{2,1,0:T(1,128)S(1)}, u32[]{:S(2)}, u32[]{:S(2)}) async-start(f32[8,1,24576]{2,1,0:T(1,128)} %reshape.240), calls=%async_computation.4 | async-start | bytes 1572864 | tf_op jit(solution)/shard_map/all_to_all | solution.py:146
  321.5 11.2 %all-to-all-done.4 = f32[8,1,24576]{2,1,0:T(1,128)S(1)} async-done(((f32[8,1,24576]{2,1,0:T(1,128)}), f32[8,1,24576]{2,1,0:T(1,128)S(1)}, u32[]{:S(2)}, u32[]{:S(2)}) %all-to-all-start.4) | async-done | bytes 786464 | tf_op jit(solution)/shard_map/all_to_all | solution.py:146
  337.5 4.4 reduce.6
  355.8 52.5 %all-to-all-done.7 = f32[48,64,192]{2,1,0:T(8,128)S(1)} async-done(((f32[48,64,192]{2,1,0:T(8,128)}), f32[48,64,192]{2,1,0:T(8,128)S(1)}, u32[]{:S(2)}, u32[]{:S(2)}) %all-to-all-start.7) | async-done | bytes 2359328 | tf_op jit(solution)/shard_map/all_to_all | solution.py:170
  408.3 4.8 all-to-all-start.5
  416.6 4.3 broadcast_in_dim.68
  420.9 96.0 %all-to-all-done.5 = f32[48,64,384]{2,1,0:T(8,128)} async-done(((f32[48,64,384]{2,1,0:T(8,128)}), f32[48,64,384]{2,1,0:T(8,128)}, u32[]{:S(2)}, u32[]{:S(2)}) %all-to-all-start.5) | async-done | bytes 4718624 | tf_op jit(solution)/shard_map/all_to_all | solution.py:169
  516.9 7.2 %copy.75 = f32[6,64,8,384]{3,2,1,0:T(8,128)} copy(f32[6,64,8,384]{3,1,0,2:T(8,128)} %bitcast.39) | data formatting | bytes 9437184 | tf_op jit(solution)/shard_map/all_to_all | solution.py:169
  524.1 5.8 %broadcast_in_dim.66 = f32[1,6,64,3072]{3,2,1,0:T(8,128)} reshape(f32[6,64,8,384]{3,2,1,0:T(8,128)} %copy.75) | data formatting | bytes 9437184 | tf_op jit(solution)/shard_map/broadcast_in_dim | solution.py:172
  (127 shorter events, 94.6 us)
Async XLA Ops:
  7.2 242.8 %all-gather.3.cloned.1.call-start = ((), (), s32[]{:S(2)}) async-start(), calls=%async_computation.8 | async-start | bytes 10616832 | tf_op jit(solution)/shard_map/all_gather | solution.py:90
  17.0 67.0 %all-to-all-start = ((bf16[8,2,36864]{2,1,0:T(2,128)(2,1)}), bf16[8,2,36864]{2,1,0:T(2,128)(2,1)S(1)}, u32[]{:S(2)}, u32[]{:S(2)}) async-start(bf16[8,2,36864]{2,1,0:T(2,128)(2,1)} %reshape.236), calls=%async_computation | async-start | bytes 2359296 | tf_op jit(solution)/shard_map/all_to_all | solution.py:99
  45.3 44.8 %copy-start.27 = (s32[48]{0:T(128)S(1)}, s32[48]{0:T(128)}, u32[]{:S(2)}) copy-start(s32[48]{0:T(128)} %param.19) | copy-start | bytes 580
  45.3 44.8 %copy-start.28 = (s32[8]{0:T(128)S(1)}, s32[8]{0:T(128)}, u32[]{:S(2)}) copy-start(s32[8]{0:T(128)} %param.18) | copy-start | bytes 100
  45.3 45.5 %copy-start.10 = (f32[128,3072]{1,0:T(8,128)S(1)}, f32[128,3072]{1,0:T(8,128)}, u32[]{:S(2)}) copy-start(f32[128,3072]{1,0:T(8,128)} %param.12) | copy-start | bytes 4718596
  85.0 115.5 %all-to-all-start.2 = ((bf16[8,2,73728]{2,1,0:T(2,128)(2,1)}), bf16[8,2,73728]{2,1,0:T(2,128)(2,1)}, u32[]{:S(2)}, u32[]{:S(2)}) async-start(bf16[8,2,73728]{2,1,0:T(2,128)(2,1)} %reshape.238), calls=%async_computation.2 | async-start | bytes 4718592 | tf_op jit(solution)/shard_map/all_to_all | solution.py:98
  99.2 110.6 %copy-start = (bf16[128,3072]{1,0:T(8,128)(2,1)S(1)}, bf16[128,3072]{1,0:T(8,128)(2,1)}, u32[]{:S(2)}) copy-start(bf16[128,3072]{1,0:T(8,128)(2,1)} %param.11) | copy-start | bytes 2359300
  200.6 31.0 %all-to-all-start.1 = ((bf16[8,64,192]{2,1,0:T(8,128)(2,1)}), bf16[8,64,192]{2,1,0:T(8,128)(2,1)S(1)}, u32[]{:S(2)}, u32[]{:S(2)}) async-start(bf16[8,64,192]{2,1,0:T(8,128)(2,1)} %gather_fusion), calls=%async_computation.1 | async-start | bytes 524288 | tf_op jit(solution)/shard_map/all_to_all | solution.py:103
  213.5 24.0 %copy-start.22 = (f32[128]{0:T(128)}, f32[128]{0:T(128)S(1)}, u32[]{:S(2)}) copy-start(f32[128]{0:T(128)S(1)} %fusion.20) | copy-start | bytes 1540
  228.4 9.2 %copy-start.1 = (f32[1,128,3072]{2,1,0:T(8,128)S(1)}, f32[1,128,3072]{2,1,0:T(8,128)}, u32[]{:S(2)}) copy-start(f32[1,128,3072]{2,1,0:T(8,128)} %get-tuple-element.7) | copy-start | bytes 4718596
  231.5 17.1 %all-to-all-start.3 = ((bf16[8,64,384]{2,1,0:T(8,128)(2,1)}), bf16[8,64,384]{2,1,0:T(8,128)(2,1)S(1)}, u32[]{:S(2)}, u32[]{:S(2)}) async-start(bf16[8,64,384]{2,1,0:T(8,128)(2,1)} %gather_fusion.1), calls=%async_computation.3 | async-start | bytes 786432 | tf_op jit(solution)/shard_map/all_to_all | solution.py:102
  237.5 11.9 %copy-start.19 = (f32[1,3072]{1,0:T(1,128)S(1)}, f32[1,3072]{1,0:T(1,128)}, u32[]{:S(2)}) copy-start(f32[1,3072]{1,0:T(1,128)} %param.14) | copy-start | bytes 36868
  237.6 12.4 %copy-start.30 = (f32[128]{0:T(128)}, f32[128]{0:T(128)S(1)}, u32[]{:S(2)}) copy-start(f32[128]{0:T(128)S(1)} %add_rsqrt_fusion.1) | copy-start | bytes 1540
  241.2 17.0 %copy-start.8 = (bf16[64,1536]{1,0:T(8,128)(2,1)}, bf16[64,1536]{1,0:T(8,128)(2,1)S(1)}, u32[]{:S(2)}) copy-start(bf16[64,1536]{1,0:T(8,128)(2,1)S(1)} %reshape.210) | copy-start | bytes 589828
  256.9 4.8 collective-permute-start
  264.5 4.6 collective-permute-start.1
  272.8 12.5 %copy-start.9 = (bf16[64,1536]{1,0:T(8,128)(2,1)S(1)}, bf16[64,1536]{1,0:T(8,128)(2,1)}, u32[]{:S(2)}) copy-start(bf16[64,1536]{1,0:T(8,128)(2,1)} %copy-done.8) | copy-start | bytes 589828
  272.8 12.5 %copy-start.21 = (f32[1,3072]{1,0:T(1,128)S(1)}, f32[1,3072]{1,0:T(1,128)}, u32[]{:S(2)}) copy-start(f32[1,3072]{1,0:T(1,128)} %param.14) | copy-start | bytes 36868
  272.8 12.5 %copy-start.26 = (f32[128]{0:T(128)S(1)}, f32[128]{0:T(128)}, u32[]{:S(2)}) copy-start(f32[128]{0:T(128)} %get-tuple-element.11) | copy-start | bytes 1540
  272.8 12.5 %copy-start.31 = (f32[128]{0:T(128)S(1)}, f32[128]{0:T(128)}, u32[]{:S(2)}) copy-start(f32[128]{0:T(128)} %copy-done.30) | copy-start | bytes 1540
  281.2 24.8 %all-to-all-start.6 = ((f32[8,1,12288]{2,1,0:T(1,128)}), f32[8,1,12288]{2,1,0:T(1,128)}, u32[]{:S(2)}, u32[]{:S(2)}) async-start(f32[8,1,12288]{2,1,0:T(1,128)} %reshape.242), calls=%async_computation.6 | async-start | bytes 786432 | tf_op jit(solution)/shard_map/all_to_all | solution.py:147
  305.9 26.8 %all-to-all-start.4 = ((f32[8,1,24576]{2,1,0:T(1,128)}), f32[8,1,24576]{2,1,0:T(1,128)S(1)}, u32[]{:S(2)}, u32[]{:S(2)}) async-start(f32[8,1,24576]{2,1,0:T(1,128)} %reshape.240), calls=%async_computation.4 | async-start | bytes 1572864 | tf_op jit(solution)/shard_map/all_to_all | solution.py:146
  333.6 74.7 %all-to-all-start.7 = ((f32[48,64,192]{2,1,0:T(8,128)}), f32[48,64,192]{2,1,0:T(8,128)S(1)}, u32[]{:S(2)}, u32[]{:S(2)}) async-start(f32[48,64,192]{2,1,0:T(8,128)} %copy.79), calls=%async_computation.7 | async-start | bytes 6291456 | tf_op jit(solution)/shard_map/all_to_all | solution.py:170
  408.3 108.6 %all-to-all-start.5 = ((f32[48,64,384]{2,1,0:T(8,128)}), f32[48,64,384]{2,1,0:T(8,128)}, u32[]{:S(2)}, u32[]{:S(2)}) async-start(f32[48,64,384]{2,1,0:T(8,128)} %copy.74), calls=%async_computation.5 | async-start | bytes 9437184 | tf_op jit(solution)/shard_map/all_to_all | solution.py:169
  (19 other events, 60.1 us)
Sparse Core Ops, SparseCore 0:
  10.2 214.7 all-gather.2
where the time goes:
time: 547 us; the launch traced here: 537 us
  waiting for transfers between devices  307 us (56%)
  local copies, waits for them, and re-layouts  107 us (20%)
  starting transfers between devices  49.1 us (9%)
  other arithmetic  36.5 us (7%)
  matrix products  21.4 us (4%)
  between operations  16.2 us (3%)
    all_to_all x1, waiting for transfers between devices, body(): lax.all_to_all(down_factors[0], 'dp', split_axis=2, concat_axis=0, tiled=...  98.6 us
    all_to_all x1, waiting for transfers between devices, body(): lax.all_to_all(slot_down, 'dp', split_axis=0, concat_axis=2, tiled=True)  96 us
    unnamed x78, local copies, waits for them, and re-layouts  54.6 us
    all_to_all x1, waiting for transfers between devices, body(): lax.all_to_all(slot_up, 'dp', split_axis=0, concat_axis=2, tiled=True)  52.5 us
    all_to_all x1, waiting for transfers between devices, body(): lax.all_to_all(up_factors[0], 'dp', split_axis=2, concat_axis=0, tiled=True)  38.7 us
    unnamed x2, other arithmetic  20.7 us
    all_to_all x1, waiting for transfers between devices, body(): lax.all_to_all(sum_down, 'dp', split_axis=2, concat_axis=0, tiled=True)  11.2 us
  transfers between devices with their start and end apart: 11, of which 7 were waited for; matrix products, arithmetic and copies ran while one was open for 24% of the time, Pallas kernels for 0%

commit v1 on v0

v1 whole, which is shorter than its diff:
```python
import jax
import jax.numpy as jnp
from jax import lax
from jax.sharding import PartitionSpec as P

epsilon = 1e-06
f32 = jnp.float32
bf16 = jnp.bfloat16


def dot(left, right, dims):
    return lax.dot_general(left, right, (dims, ((), ())), preferred_element_type=f32)


def body(
    latents,
    out_grad,
    frozen_weight,
    norm_gain,
    time_gate,
    down_factors,
    up_factors,
    block_jobs,
    owners,
    block_steps,
    block_fill,
):
    is_first = lax.axis_index("section") == 0
    place = lax.axis_index("dp")
    slot_local, low_rank, width = down_factors.shape[1:]
    out_width = up_factors.shape[3]
    blocks_dev = block_fill.shape[0]
    rows = latents.shape[0] // blocks_dev
    gain = norm_gain[0]
    gate = time_gate[0]

    frozen = lax.all_gather(frozen_weight[0], "dp", axis=0, tiled=True)

    matches = block_jobs[:, None] == jnp.arange(owners.shape[0], dtype=jnp.int32)[None, :]
    slot_of = jnp.sum(jnp.where(matches, owners[None, :], 0), axis=1)
    first_slot = place * slot_local
    mine = [(slot_of == first_slot + j)[:, None, None] for j in range(slot_local)]

    def spread(factors):
        total = jnp.zeros((), bf16)
        for j in range(slot_local):
            total = jnp.where(mine[j], factors[j][None], total)
        return total

    down = lax.psum_scatter(spread(down_factors[0]), "dp", scatter_dimension=0, tiled=True)
    up = lax.psum_scatter(spread(up_factors[0]), "dp", scatter_dimension=0, tiled=True)

    chosen = block_steps[:, None] == jnp.arange(gate.shape[0], dtype=jnp.int32)[None, :]
    scales = jnp.sum(jnp.where(chosen, gate[None, :], 0.0), axis=1)
    row_scale = jnp.repeat(scales, rows)[:, None]
    live = (jnp.arange(rows, dtype=jnp.int32)[None, :] < block_fill[:, None]).reshape(-1, 1)
    masked = jnp.where(live, out_grad, 0.0)

    def per_block(left, right, dims):
        left = left.reshape(blocks_dev, -1, left.shape[-1])
        return [dot(left[b], right[b], dims) for b in range(blocks_dev)]

    def forward(x):
        values = x.astype(f32)
        inverse = lax.rsqrt(jnp.mean(values * values, axis=1, keepdims=True) + epsilon)
        normed = (values * inverse * gain[None, :]).astype(bf16)
        low = jnp.concatenate(per_block(normed, down, ((1,), (1,)))).astype(bf16)
        return values, inverse, normed, low

    def layer_out(x, values, normed, low):
        extra = jnp.concatenate(per_block(low, up, ((1,), (0,))))
        update = row_scale * (dot(normed, frozen, ((1,), (0,))) + extra)
        return (values[:, :out_width] + update).astype(bf16)

    pair = [(0, 1)]
    values, inverse, normed, low = forward(latents)
    window = layer_out(latents, values, normed, low)
    window = lax.ppermute(window, "section", pair)
    x = jnp.where(is_first, latents, jnp.concatenate([window, latents[:, out_width:]], axis=1))
    values, inverse, normed, low = forward(x)

    head = masked[:, :out_width]
    delta = (row_scale * head).astype(bf16)
    low_grad = jnp.concatenate(per_block(delta, up, ((1,), (1,)))).astype(bf16)
    norm_grad = dot(delta, frozen, ((1,), (1,))) + jnp.concatenate(
        per_block(low_grad, down, ((1,), (0,)))
    )
    scaled = gain[None, :] * norm_grad
    inner = jnp.mean(values * scaled, axis=1, keepdims=True)
    cubed = inverse * inverse * inverse
    carried = (
        head
        + inverse * scaled[:, :out_width]
        - values[:, :out_width] * (cubed * inner)
    ).astype(bf16)
    carried = lax.ppermute(carried, "section", [(1, 0)])
    head = jnp.where(is_first, carried.astype(f32), head)
    delta = (row_scale * head).astype(bf16)
    low_grad = jnp.concatenate(per_block(delta, up, ((1,), (1,)))).astype(bf16)

    def outer(left, right):
        left = left.reshape(blocks_dev, rows, -1)
        right = right.reshape(blocks_dev, rows, -1)
        return jnp.stack([dot(left[b], right[b], ((0,), (0,))) for b in range(blocks_dev)])

    grad_down = outer(low_grad, normed).astype(bf16)
    grad_up = outer(low, delta).astype(bf16)
    all_down = lax.all_gather(grad_down, "dp", axis=0, tiled=True)
    all_up = lax.all_gather(grad_up, "dp", axis=0, tiled=True)

    def gather_slots(grads):
        slots = []
        for j in range(slot_local):
            slots.append(jnp.sum(jnp.where(mine[j], grads.astype(f32), 0.0), axis=0))
        return jnp.stack(slots)[None]

    return gather_slots(all_down), gather_slots(all_up)


def solution(mesh):
    placed = (
        P(("groups", "dp"), None),
        P(("groups", "dp"), None),
        P("section", "dp", None),
        P("section", None),
        P("section", None),
        P("section", ("groups", "dp"), None, None),
        P("section", ("groups", "dp"), None, None),
        P("groups"),
        P("groups"),
        P(("groups", "dp")),
        P(("groups", "dp")),
    )
    return jax.shard_map(
        body,
        mesh=mesh,
        in_specs=placed,
        out_specs=(
            P("section", ("groups", "dp"), None, None),
            P("section", ("groups", "dp"), None, None),
        ),
        check_vma=False,
    )
```

time: 547 us -> 444 us (0.81); the launches traced: 537 us -> 444 us
  local copies, waits for them, and re-layouts: 107 us -> 5.31 us
  waiting for transfers between devices: 307 us -> 376 us
  starting transfers between devices: 49.1 us -> 3.99 us
  other arithmetic: 36.5 us -> 19.1 us
    all_to_all x8 -> x0, waiting for transfers between devices: 304 us -> none  [the longest x1 98.6 us: body(): lax.all_to_all(down_factors[0], 'dp', split_axis=2, concat_axis=0, tiled=...]
    all_gather x1 -> x3, waiting for transfers between devices: 0.02 us -> 233 us  [the longest x1 133 us: body(): frozen = lax.all_gather(frozen_weight[0], 'dp', axis=0, tiled=True)]
    reduce_scatter x0 -> x2, waiting for transfers between devices: none -> 140 us  [the longest x1 77.9 us: body(): lax.psum_scatter(spread(down_factors[0]), 'dp', scatter_dimension=0, tile...]
    unnamed x78 -> x58, local copies, waits for them, and re-layouts: 54.6 us -> 4.98 us
    all_to_all x8 -> x0, starting transfers between devices: 46.1 us -> none  [the longest x1 9.28 us: body(): lax.all_to_all(spread_up[slot_of], 'dp', split_axis=0, concat_axis=2, til...]
    all_to_all x7 -> x0, local copies, waits for them, and re-layouts: 24.9 us -> none  [the longest x1 7.2 us: body(): lax.all_to_all(slot_down, 'dp', split_axis=0, concat_axis=2, tiled=True)]
    unnamed x2 -> x0, other arithmetic: 20.7 us -> none
    reduce_sum x2 -> x4, other arithmetic: 0.89 us -> 10.7 us  [the longest x2 9.83 us: gather_slots(): slots.append(jnp.sum(jnp.where(mine[j], grads.astype(f32), 0.0), axis=0))]
  transfers between devices with their start and end apart: 11 -> 7, of which waited for: 7 -> 6; matrix products, arithmetic and copies ran while one was open for 24% -> 6% of each run, Pallas kernels for 0% -> 0%
where the time goes in v1:
time: 444 us
  waiting for transfers between devices  376 us (85%)
  matrix products  23.8 us (5%)
  other arithmetic  19.1 us (4%)
  between operations  15.5 us (3%)
  local copies, waits for them, and re-layouts  5.31 us (1%)
    all_gather x1, waiting for transfers between devices, body(): frozen = lax.all_gather(frozen_weight[0], 'dp', axis=0, tiled=True)  133 us
    reduce_scatter x1, waiting for transfers between devices, body(): lax.psum_scatter(spread(down_factors[0]), 'dp', scatter_dimension=0, tile...  77.9 us
    reduce_scatter x1, waiting for transfers between devices, body(): lax.psum_scatter(spread(up_factors[0]), 'dp', scatter_dimension=0, tiled=...  61.9 us
    all_gather x1, waiting for transfers between devices, body(): all_down = lax.all_gather(grad_down, 'dp', axis=0, tiled=True)  57.9 us
    all_gather x1, waiting for transfers between devices, body(): all_up = lax.all_gather(grad_up, 'dp', axis=0, tiled=True)  42.1 us
    dot_general x6, matrix products, dot(): lax.dot_general(left, right, (dims, ((), ())), preferred_element_type=f32)  23.8 us
    reduce_sum x2, other arithmetic, gather_slots(): slots.append(jnp.sum(jnp.where(mine[j], grads.astype(f32), 0.0), axis=0))  9.83 us
  transfers between devices with their start and end apart: 7, of which 6 were waited for; matrix products, arithmetic and copies ran while one was open for 6% of the time, Pallas kernels for 0%

profile of v1, /device:TPU:0, one launch (start us, length us, event | category | flops | bytes accessed | tf_op | source)
XLA Modules:
  0.0 443.8 jit_solution(14806286856452990832)
XLA Ops:
  8.0 0.9 select_reduce_fusion
  9.0 1.8 select_select_fusion.1
  11.1 2.6 select_select_fusion
  13.8 1.0 copy-done
  17.7 133.3 %all-gather.7.cloned.1.call-done = bf16[1,3072,1536]{2,1,0:T(8,128)(2,1)} async-done(((bf16[1,384,1536]{2,1,0:T(8,128)(2,1)}), bf16[1,3072,1536]{2,1,0:T(8,128)(2,1)}) %all-gather.7.cloned.1.call-update) | async-done | bytes 9437200 | tf_op jit(solution)/shard_map/all_gather | solution.py:37
  151.0 5.1 %fusion.2 = f32[128,1536]{1,0:T(8,128)S(1)} fusion(bf16[1,3072,1536]{2,1,0:T(8,128)(2,1)} %all-gather.7.cloned.1.call-done, f32[3072]{0:T(1024)S(1)} %bitcast.90, f32[128]{0:T(128)S(1)} %add_rsqrt_fusion.1, bf16[128,3072]{1,0:T(8,128)(2,1)S(1)} %copy-done), kind=kOutput, calls=%fused_computation.8 | convolution fusion | flops 1209532416 | bytes 11022848 | tf_op jit(solution)/shard_map/dot_general | solution.py:12
  156.1 61.9 %reduce-scatter.5.cloned.1.call-done = bf16[1,64,1536]{2,1,0:T(8,128)(2,1)} async-done(((bf16[8,64,1536]{2,1,0:T(8,128)(2,1)}), bf16[1,64,1536]{2,1,0:T(8,128)(2,1)}) %reduce-scatter.5.cloned.1.call-update) | async-done | bytes 196624 | tf_op jit(solution)/shard_map/reduce_scatter | solution.py:51
  218.0 77.9 %reduce-scatter.3.cloned.1.call-done = bf16[1,64,3072]{2,1,0:T(8,128)(2,1)} async-done(((bf16[8,64,3072]{2,1,0:T(8,128)(2,1)}), bf16[1,64,3072]{2,1,0:T(8,128)(2,1)}) %reduce-scatter.3.cloned.1.call-update) | async-done | bytes 393232 | tf_op jit(solution)/shard_map/reduce_scatter | solution.py:50
  295.9 3.3 fusion.19
  299.2 2.2 collective-permute-start
  301.4 7.8 %fusion = f32[128,3072]{1,0:T(8,128)S(1)} fusion(bf16[1,3072,1536]{2,1,0:T(8,128)(2,1)} %all-gather.7.cloned.1.call-done, f32[128,3072]{1,0:T(8,128)} %param.12, f32[]{:T(128)} %fusion.34, pred[128]{0:T(512)(128)(4,1)} %iota_compare_fusion.1), kind=kOutput, calls=%fused_computation.6 | convolution fusion | flops 1208549376 | bytes 11797504 | tf_op jit(solution)/shard_map/dot_general | solution.py:12
  309.2 4.8 %multiply_reduce_fusion.1 = (f32[128]{0:T(128)}, f32[128]{0:T(128)}, bf16[128,3072]{1,0:T(8,128)(2,1)S(1)}, f32[128,3072]{1,0:T(8,128)}) fusion(bf16[128,3072]{1,0:T(8,128)(2,1)S(1)} %copy-done.1, bf16[128,1536]{1,0:T(8,128)(2,1)S(1)} %slice-done, bf16[128,1536]{1,0:T(8,128)(2,1)} %collective-permute-done, pred[]{:T(512)S(6)} %eq.102, ...), kind=kOutput, calls=%fused_computation.39 | convolution fusion | flops 80813824 | bytes 6895617 | tf_op jit(solution)/shard_map/dot_general | solution.py:12
  314.7 0.7 copy-done.2
  315.4 1.4 fusion.21
  316.8 1.4 collective-permute-start.1
  318.3 2.3 collective-permute-done.1
  320.6 0.9 multiply_convert_fusion.2
  321.5 1.4 convolution_convert_fusion.1
  323.1 1.4 convolution_convert_fusion
  324.6 42.1 %all-gather.11.cloned.1.call-done = bf16[512,1536]{1,0:T(8,128)(2,1)} async-done(((bf16[64,1536]{1,0:T(8,128)(2,1)}), bf16[512,1536]{1,0:T(8,128)(2,1)}) %all-gather.11.cloned.1.call-update) | async-done | bytes 1572880 | tf_op jit(solution)/shard_map/all_gather | solution.py:109
  366.7 3.9 fusion.16
  370.9 57.9 %all-gather.9.cloned.1.call-done = bf16[512,3072]{1,0:T(8,128)(2,1)} async-done(((bf16[64,3072]{1,0:T(8,128)(2,1)}), bf16[512,3072]{1,0:T(8,128)(2,1)}) %all-gather.9.cloned.1.call-update) | async-done | bytes 3145744 | tf_op jit(solution)/shard_map/all_gather | solution.py:108
  428.8 5.9 %fusion.9 = (f32[64,3072]{1,0:T(8,128)S(1)}, f32[64,3072]{1,0:T(8,128)S(1)}, f32[64,3072]{1,0:T(8,128)S(1)}, f32[64,3072]{1,0:T(8,128)S(1)}, f32[64,3072]{1,0:T(8,128)S(1)}, /*index=5*/f32[64,3072]{1,0:T(8,128)S(1)}) fusion(bf16[8,64,3072]{2,1,0:T(8,128)(2,1)} %bitcast.88, pred[8]{0:T(512)(128)(4,1)S(1)} %copy-done.19, pred[8]{0:T(512)(128)(4,1)S(1)} %copy-done.11, ...), kind=kLoop, calls=%fused_computation.21 | loop fusion | flops 19267584 | bytes 7864368 | tf_op jit(solution)/shard_map/reduce_sum | solution.py:114
  435.1 2.2 copy-done.8
  (80 shorter events, 4.2 us)
Async XLA Ops:
  7.2 143.8 %all-gather.7.cloned.1.call-start = ((), (), s32[]{:S(2)}) async-start(), calls=%async_computation.4 | async-start | bytes 10616832 | tf_op jit(solution)/shard_map/all_gather | solution.py:37
  7.9 210.1 %reduce-scatter.5.cloned.1.call-start = ((), (), s32[]{:S(2)}) async-start(), calls=%async_computation.3 | async-start | bytes 1769472 | tf_op jit(solution)/shard_map/reduce_scatter | solution.py:51
  8.8 2.2 copy-start.10
  8.8 2.2 copy-start.12
  8.9 2.2 copy-start.14
  8.9 2.2 copy-start.16
  10.8 285.1 %reduce-scatter.3.cloned.1.call-start = ((), (), s32[]{:S(2)}) async-start(), calls=%async_computation.2 | async-start | bytes 3538944 | tf_op jit(solution)/shard_map/reduce_scatter | solution.py:50
  13.7 353.0 %all-gather.11.cloned.1.call-start = ((), (), s32[]{:S(2)}) async-start(), calls=%async_computation.6 | async-start | bytes 1769472 | tf_op jit(solution)/shard_map/all_gather | solution.py:109
  13.7 3.0 copy-start.23
  14.8 136.2 %copy-start.7 = (f32[1,3072]{1,0:T(1,128)S(1)}, f32[1,3072]{1,0:T(1,128)}, u32[]{:S(2)}) copy-start(f32[1,3072]{1,0:T(1,128)} %param.14) | copy-start | bytes 36868
  299.2 10.0 %copy-start.1 = (bf16[128,3072]{1,0:T(8,128)(2,1)S(1)}, bf16[128,3072]{1,0:T(8,128)(2,1)}, u32[]{:S(2)}) copy-start(bf16[128,3072]{1,0:T(8,128)(2,1)} %param.11) | copy-start | bytes 2359300
  299.2 10.0 %slice-start = ((bf16[128,3072]{1,0:T(8,128)(2,1)}), bf16[128,1536]{1,0:T(8,128)(2,1)S(1)}, s32[]{:S(2)}) async-start(bf16[128,3072]{1,0:T(8,128)(2,1)} %param.11), calls=%async_computation.7 | async-start | bytes 786432 | tf_op jit(solution)/shard_map/slice | solution.py:79
  299.2 10.0 %collective-permute-start = (bf16[128,1536]{1,0:T(8,128)(2,1)}, bf16[128,1536]{1,0:T(8,128)(2,1)}, u32[]{:S(2)}, u32[]{:S(2)}) collective-permute-start(bf16[128,1536]{1,0:T(8,128)(2,1)} %fusion.19), channel_id=1, source_target_pairs={{0,1},{2,3},{4,5},{6,7},{8,9},{10,11},{12,13},{14,15},{16,17},{18,... | collective-permute-start | bytes 1179656 | tf_op jit(solution)/shard_map/ppermute | solution.py:78
  315.4 6.1 %copy-start.5 = (bf16[1,64,3072]{2,1,0:T(8,128)(2,1)S(1)}, bf16[1,64,3072]{2,1,0:T(8,128)(2,1)}, u32[]{:S(2)}) copy-start(bf16[1,64,3072]{2,1,0:T(8,128)(2,1)} %reduce-scatter.3.cloned.1.call-done) | copy-start | bytes 1179652
  316.8 6.3 %copy-start.4 = (bf16[1,64,1536]{2,1,0:T(8,128)(2,1)S(1)}, bf16[1,64,1536]{2,1,0:T(8,128)(2,1)}, u32[]{:S(2)}) copy-start(bf16[1,64,1536]{2,1,0:T(8,128)(2,1)} %reduce-scatter.5.cloned.1.call-done) | copy-start | bytes 589828
  316.8 3.7 collective-permute-start.1
  322.9 43.8 %copy-start.11 = (pred[8]{0:T(512)(128)(4,1)S(1)}, pred[8]{0:T(512)(128)(4,1)}, u32[]{:S(2)}) copy-start(pred[8]{0:T(512)(128)(4,1)} %copy-done.10) | copy-start | bytes 28
  322.9 43.8 %copy-start.13 = (pred[8]{0:T(512)(128)(4,1)S(1)}, pred[8]{0:T(512)(128)(4,1)}, u32[]{:S(2)}) copy-start(pred[8]{0:T(512)(128)(4,1)} %copy-done.12) | copy-start | bytes 28
  322.9 43.8 %copy-start.15 = (pred[8]{0:T(512)(128)(4,1)S(1)}, pred[8]{0:T(512)(128)(4,1)}, u32[]{:S(2)}) copy-start(pred[8]{0:T(512)(128)(4,1)} %copy-done.14) | copy-start | bytes 28
  322.9 43.8 %copy-start.17 = (pred[8]{0:T(512)(128)(4,1)S(1)}, pred[8]{0:T(512)(128)(4,1)}, u32[]{:S(2)}) copy-start(pred[8]{0:T(512)(128)(4,1)} %copy-done.16) | copy-start | bytes 28
  322.9 43.8 %copy-start.19 = (pred[8]{0:T(512)(128)(4,1)S(1)}, pred[8]{0:T(512)(128)(4,1)}, u32[]{:S(2)}) copy-start(pred[8]{0:T(512)(128)(4,1)} %copy-done.18) | copy-start | bytes 28
  322.9 105.9 %all-gather.9.cloned.1.call-start = ((), (), s32[]{:S(2)}) async-start(), calls=%async_computation.5 | async-start | bytes 3538944 | tf_op jit(solution)/shard_map/all_gather | solution.py:108
  370.8 63.9 %copy-start.9 = (f32[6,64,1536]{2,1,0:T(8,128)}, f32[6,64,1536]{2,1,0:T(8,128)S(1)}, u32[]{:S(2)}) copy-start(f32[6,64,1536]{2,1,0:T(8,128)S(1)} %bitcast_dynamic-update-slice_fusion.6) | copy-start | bytes 7077892
  435.1 2.2 copy-start.8
  (8 other events, 11.0 us)
Sparse Core Ops, SparseCore 0:
  10.2 140.7 all-gather.6
  155.0 62.9 reduce-scatter.4
  222.6 73.2 reduce-scatter.2
  323.0 43.5 all-gather.10
  369.5 59.2 all-gather.8

commit v2 on v1

--- a/solution.py
+++ b/solution.py
@@ -1,6 +1,10 @@
+import functools
+
 import jax
 import jax.numpy as jnp
 from jax import lax
+from jax.experimental import pallas as pl
+from jax.experimental.pallas import tpu as pltpu
 from jax.sharding import PartitionSpec as P
 
 epsilon = 1e-06
@@ -10,6 +14,199 @@
 
 def dot(left, right, dims):
     return lax.dot_general(left, right, (dims, ((), ())), preferred_element_type=f32)
+
+
+MESH = pl.DeviceIdType.MESH
+
+
+def ring_index(spot, n):
+    spot = lax.rem(spot + 2 * n, n)
+    half = (n + 1) // 2
+    return jnp.where(spot < half, 2 * spot, 2 * (n - 1 - spot) + 1)
+
+
+def ring_spot(index, n):
+    return jnp.where(lax.rem(index, 2) == 0, index // 2, n - 1 - index // 2)
+
+
+def remote(src, dst, send, recv, **where):
+    return pltpu.make_async_remote_copy(
+        src_ref=src,
+        dst_ref=dst,
+        send_sem=send,
+        recv_sem=recv,
+        device_id=where,
+        device_id_type=MESH,
+    )
+
+
+def greet(*places):
+    barrier = pltpu.get_barrier_semaphore()
+    for where in places:
+        pl.semaphore_signal(barrier, inc=1, device_id=where, device_id_type=MESH)
+    pl.semaphore_wait(barrier, len(places))
+
+
+def fetch_kernel(
+    n, w_ref, f_ref, w_out, f_out, acc, own, w_send, w_recv, y_send, y_recv, f_send, f_recv, local
+):
+    depth = w_ref.shape[0]
+    quarter = depth // 4
+    half = f_ref.shape[1] // 2
+    plane = lax.axis_index("groups")
+    p = ring_spot(lax.axis_index("dp"), n)
+    nexts = (ring_index(p + 1, n), ring_index(p - 1, n))
+    greet({"dp": nexts[0]}, {"dp": nexts[1]}, {"groups": 1 - plane})
+
+    def piece(owner, part):
+        start = pl.multiple_of(owner * depth + part * quarter, quarter)
+        return w_out.at[pl.ds(start, quarter)]
+
+    def w_copy(way, step):
+        part = 2 * plane + way
+        owner = ring_index(p - step if way == 0 else p + step, n)
+        target = piece(owner, part)
+        start = pl.multiple_of(part * quarter, quarter)
+        source = w_ref.at[pl.ds(start, quarter)] if step == 0 else target
+        return remote(
+            source, target, w_send.at[way, step], w_recv.at[way, step], dp=nexts[way]
+        )
+
+    def w_arrival(way, step):
+        owner = ring_index(p - 1 - step if way == 0 else p + 1 + step, n)
+        target = piece(owner, 2 * plane + way)
+        return remote(
+            target, target, w_send.at[way, step], w_recv.at[way, step], dp=nexts[way]
+        )
+
+    def y_copy(way, step, part):
+        owner = ring_index(p - 1 - step if way == 0 else p + 1 + step, n)
+        target = piece(owner, part)
+        return remote(
+            target, target, y_send.at[way, step], y_recv.at[way, step], groups=1 - plane
+        )
+
+    def f_rows(way):
+        return pl.ds(way * half, half)
+
+    def f_copy(way, step):
+        block = ring_index(p - 1 - step if way == 0 else p + 1 + step, n)
+        source = own.at[block, f_rows(way)] if step == 0 else acc.at[way, step - 1]
+        return remote(
+            source, acc.at[way, step], f_send.at[way, step], f_recv.at[way, step], dp=nexts[way]
+        )
+
+    for way in range(2):
+        w_copy(way, 0).start()
+    mine = pltpu.make_async_copy(f_ref, own, local.at[0])
+    mine.start()
+    start = pl.multiple_of(lax.axis_index("dp") * depth, depth)
+    keep = pltpu.make_async_copy(w_ref, w_out.at[pl.ds(start, depth)], local.at[1])
+    keep.start()
+    mine.wait()
+    for way in range(2):
+        f_copy(way, 0).start()
+
+    last = n - 2
+    for step in range(n - 1):
+        for way in range(2):
+            w_arrival(way, step).wait_recv()
+            if step < last:
+                w_copy(way, step + 1).start()
+            y_copy(way, step, 2 * plane + way).start()
+        for way in range(2):
+            f_copy(way, step).wait_recv()
+            block = ring_index(p - 2 - step if way == 0 else p + 2 + step, n)
+            total = acc[way, step] + own[block, f_rows(way)]
+            if step < last:
+                acc[way, step] = total
+                f_copy(way, step + 1).start()
+            else:
+                f_out[f_rows(way)] = total
+    for step in range(n - 1):
+        for way in range(2):
+            y_copy(way, step, 2 * (1 - plane) + way).wait_recv()
+            w_copy(way, step).wait_send()
+            f_copy(way, step).wait_send()
+            y_copy(way, step, 2 * plane + way).wait_send()
+    keep.wait()
+
+
+def fetch(n, w, f):
+    depth, columns = w.shape
+    blocks, rank, cut = f.shape
+    steps = (2, n - 1)
+    pairs = [pltpu.SemaphoreType.DMA(steps)] * 6
+    return pl.pallas_call(
+        functools.partial(fetch_kernel, n),
+        out_shape=(
+            jax.ShapeDtypeStruct((n * depth, columns), w.dtype),
+            jax.ShapeDtypeStruct((rank, cut), f.dtype),
+        ),
+        in_specs=[pl.BlockSpec(memory_space=pl.ANY)] * 2,
+        out_specs=(
+            pl.BlockSpec(memory_space=pl.ANY),
+            pl.BlockSpec(memory_space=pltpu.VMEM),
+        ),
+        scratch_shapes=[
+            pltpu.VMEM((2, n - 1, rank // 2, cut), f.dtype),
+            pltpu.VMEM((blocks, rank, cut), f.dtype),
+            *pairs,
+            pltpu.SemaphoreType.DMA((2,)),
+        ],
+        compiler_params=pltpu.CompilerParams(
+            collective_id=0, has_side_effects=True, vmem_limit_bytes=32 << 20
+        ),
+        name="fetch",
+    )(w, f)
+
+
+def share_kernel(n, g_ref, g_out, send, recv, local):
+    half = g_ref.shape[0] // 2
+    me = lax.axis_index("dp")
+    p = ring_spot(me, n)
+    nexts = (ring_index(p + 1, n), ring_index(p - 1, n))
+    greet({"dp": nexts[0]}, {"dp": nexts[1]})
+
+    def copy(way, step):
+        owner = ring_index(p - step if way == 0 else p + step, n)
+        part = pl.ds(way * half, half)
+        target = g_out.at[owner, part]
+        source = g_ref.at[part] if step == 0 else target
+        return remote(source, target, send.at[way, step], recv.at[way, step], dp=nexts[way])
+
+    def arrival(way, step):
+        owner = ring_index(p - 1 - step if way == 0 else p + 1 + step, n)
+        target = g_out.at[owner, pl.ds(way * half, half)]
+        return remote(target, target, send.at[way, step], recv.at[way, step], dp=nexts[way])
+
+    for way in range(2):
+        copy(way, 0).start()
+    keep = pltpu.make_async_copy(g_ref, g_out.at[me], local.at[0])
+    keep.start()
+    for step in range(n - 1):
+        for way in range(2):
+            arrival(way, step).wait_recv()
+            if step < n - 2:
+                copy(way, step + 1).start()
+    for step in range(n - 1):
+        for way in range(2):
+            copy(way, step).wait_send()
+    keep.wait()
+
+
+def share(n, g):
+    rank, cut = g.shape
+    pairs = [pltpu.SemaphoreType.DMA((2, n - 1))] * 2
+    return pl.pallas_call(
+        functools.partial(share_kernel, n),
+        out_shape=jax.ShapeDtypeStruct((n, rank, cut), g.dtype),
+        in_specs=[pl.BlockSpec(memory_space=pl.ANY)],
+        out_specs=pl.BlockSpec(memory_space=pl.ANY),
+        scratch_shapes=[*pairs, pltpu.SemaphoreType.DMA((1,))],
+        compiler_params=pltpu.CompilerParams(collective_id=1, has_side_effects=True),
+        name="share",
+    )(g)
 
 
 def body(
@@ -34,7 +231,14 @@
     gain = norm_gain[0]
     gate = time_gate[0]
 
-    frozen = lax.all_gather(frozen_weight[0], "dp", axis=0, tiled=True)
+    lanes = lax.axis_size("dp")
+    ringed = (
+        3 <= lanes <= 16
+        and lax.axis_size("groups") == 2
+        and blocks_dev == 1
+        and frozen_weight.shape[1] % 64 == 0
+        and low_rank % 32 == 0
+    )
 
     matches = block_jobs[:, None] == jnp.arange(owners.shape[0], dtype=jnp.int32)[None, :]
     slot_of = jnp.sum(jnp.where(matches, owners[None, :], 0), axis=1)
@@ -47,8 +251,15 @@
             total = jnp.where(mine[j], factors[j][None], total)
         return total
 
-    down = lax.psum_scatter(spread(down_factors[0]), "dp", scatter_dimension=0, tiled=True)
-    up = lax.psum_scatter(spread(up_factors[0]), "dp", scatter_dimension=0, tiled=True)
+    if ringed:
+        sent = jnp.concatenate([spread(down_factors[0]), spread(up_factors[0])], axis=2)
+        frozen, factors = fetch(lanes, frozen_weight[0], sent)
+        down = factors[None, :, :width]
+        up = factors[None, :, width:]
+    else:
+        frozen = lax.all_gather(frozen_weight[0], "dp", axis=0, tiled=True)
+        down = lax.psum_scatter(spread(down_factors[0]), "dp", scatter_dimension=0, tiled=True)
+        up = lax.psum_scatter(spread(up_factors[0]), "dp", scatter_dimension=0, tiled=True)
 
     chosen = block_steps[:, None] == jnp.arange(gate.shape[0], dtype=jnp.int32)[None, :]
     scales = jnp.sum(jnp.where(chosen, gate[None, :], 0.0), axis=1)
@@ -105,8 +316,12 @@
 
     grad_down = outer(low_grad, normed).astype(bf16)
     grad_up = outer(low, delta).astype(bf16)
-    all_down = lax.all_gather(grad_down, "dp", axis=0, tiled=True)
-    all_up = lax.all_gather(grad_up, "dp", axis=0, tiled=True)
+    if ringed:
+        shared = share(lanes, jnp.concatenate([grad_down[0], grad_up[0]], axis=1))
+        all_down, all_up = shared[:, :, :width], shared[:, :, width:]
+    else:
+        all_down = lax.all_gather(grad_down, "dp", axis=0, tiled=True)
+        all_up = lax.all_gather(grad_up, "dp", axis=0, tiled=True)
 
     def gather_slots(grads):
         slots = []

time: 444 us -> 212 us (0.48)
  waiting for transfers between devices: 376 us -> 2.14 us
  Pallas kernels: 0 us -> 156 us
  between operations: 15.5 us -> 2.27 us
    all_gather x3 -> x0, waiting for transfers between devices: 233 us -> none  [the longest x1 133 us: body(): frozen = lax.all_gather(frozen_weight[0], 'dp', axis=0, tiled=True)]
    pallas_call x0 -> x2, Pallas kernels: none -> 156 us  [the longest x1 102 us: fetch(): pl.pallas_call(functools.partial(fetch_kernel, n), out_shape=(jax.ShapeDt...]
    reduce_scatter x2 -> x0, waiting for transfers between devices: 140 us -> none  [the longest x1 77.9 us: body(): lax.psum_scatter(spread(down_factors[0]), 'dp', scatter_dimension=0, tile...]
  transfers between devices with their start and end apart: 7 -> 2, of which waited for: 6 -> 1; matrix products, arithmetic and copies ran while one was open for 6% -> 4% of each run, Pallas kernels for 0% -> 0%
where the time goes in v2:
time: 212 us
  Pallas kernels  156 us (74%)
  matrix products  21.2 us (10%)
  other arithmetic  19.5 us (9%)
  local copies, waits for them, and re-layouts  7.54 us (4%)
  starting transfers between devices  3.52 us (2%)
  between operations  2.27 us (1%)
  waiting for transfers between devices  2.14 us (1%)
    pallas_call x1, Pallas kernels, fetch(): pl.pallas_call(functools.partial(fetch_kernel, n), out_shape=(jax.ShapeDt...  102 us
    pallas_call x1, Pallas kernels, share(): pl.pallas_call(functools.partial(share_kernel, n), out_shape=jax.ShapeDty...  54 us
    dot_general x6, matrix products, dot(): lax.dot_general(left, right, (dims, ((), ())), preferred_element_type=f32)  21.2 us
    reduce_sum x2, other arithmetic, gather_slots(): slots.append(jnp.sum(jnp.where(mine[j], grads.astype(f32), 0.0), axis=0))  9.37 us
    unnamed x38, local copies, waits for them, and re-layouts  7.22 us
  transfers between devices with their start and end apart: 2, of which 1 were waited for; matrix products, arithmetic and copies ran while one was open for 4% of the time, Pallas kernels for 0%

profile of v2, /device:TPU:0, one launch (start us, length us, event | category | flops | bytes accessed | tf_op | source)
XLA Modules:
  0.0 212.0 jit_solution(10597924603985598472)
XLA Ops:
  0.6 1.5 multiply_reduce_fusion.2
  2.2 2.4 %convert_element_type.63 = f32[128,3072]{1,0:T(8,128)} convert(bf16[128,3072]{1,0:T(8,128)(2,1)} %param.11) | non-fusion elementwise | flops 393216 | bytes 2359296 | tf_op jit(solution)/shard_map/convert_element_type | solution.py:275
  4.8 1.1 copy-done.7
  6.8 1.0 select_select_fusion
  8.8 0.9 copy-done.1
  9.7 101.8 %fetch.1 = (bf16[3072,1536]{1,0:T(8,128)(2,1)S(1)}, bf16[64,4608]{1,0:T(8,128)(2,1)S(1)}) custom-call(bf16[384,1536]{1,0:T(8,128)(2,1)S(1)} %bitcast.60, bf16[8,64,4608]{2,1,0:T(8,128)(2,1)S(1)} %pad_maximum_fusion.f_ref), custom_call_target="tpu_custom_call" | custom-call | tf_op jit(solution)/shard_map/fetch/pallas_call | solution.py:140
  111.6 0.8 fusion.31
  112.3 2.9 %fusion.24 = f32[128,1536]{1,0:T(8,128)} fusion(bf16[3072,1536]{1,0:T(8,128)(2,1)S(1)} %get-tuple-element.4, f32[3072]{0:T(1024)S(1)} %bitcast.61, f32[128]{0:T(128)S(1)} %add_rsqrt_fusion.1, bf16[128,3072]{1,0:T(8,128)(2,1)S(1)} %copy-done.2), kind=kOutput, calls=%fused_computation.75 | convolution fusion | flops 1209532416 | bytes 11022848 | tf_op jit(solution)/shard_map/dot_general | solution.py:16
  115.4 3.7 %fusion.15 = bf16[128,1536]{1,0:T(8,128)(2,1)} fusion(f32[128,1536]{1,0:T(8,128)} %fusion.24, f32[128,3072]{1,0:T(8,128)} %convert_element_type.63, f32[]{:T(128)} %fusion.31, bf16[64,4608]{1,0:T(8,128)(2,1)S(1)} %get-tuple-element.5, f32[3072]{0:T(1024)S(1)} %bitcast.62, f32[128]{0:T(128)S(1)} %add_rsqrt_fusion.1, bf16[128,3072]{1,0:T(8,128)(2,1)S(1)} %copy-done.2), kind=kOutput, calls=%fused_computation.32 | convolution fusion | flops 77864960 | bytes 3355140 | tf_op jit(solution)/shard_map/dot_general | solution.py:16
  119.1 2.0 collective-permute-start
  121.8 8.7 %fusion.32 = f32[128,3072]{1,0:T(8,128)} fusion(bf16[3072,1536]{1,0:T(8,128)(2,1)} %copy-done, f32[128,3072]{1,0:T(8,128)S(1)} %copy-done.4, f32[]{:T(128)} %fusion.31, pred[128]{0:T(512)(128)(4,1)S(1)} %iota_compare_fusion.1), kind=kOutput, calls=%fused_computation.100 | convolution fusion | flops 1208549376 | bytes 11796996 | tf_op jit(solution)/shard_map/dot_general | solution.py:16
  130.6 4.5 %multiply_reduce_fusion.1 = (f32[128]{0:T(128)S(1)}, f32[128]{0:T(128)S(1)}, bf16[128,3072]{1,0:T(8,128)(2,1)S(1)}, f32[128,3072]{1,0:T(8,128)}) fusion(bf16[128,3072]{1,0:T(8,128)(2,1)S(1)} %copy-done.3, bf16[128,1536]{1,0:T(8,128)(2,1)S(1)} %slice-done, bf16[128,1536]{1,0:T(8,128)(2,1)} %collective-permute-done, pred[]{:T(512)S(6)} %eq.102, ...), kind=kOutput, calls=%fused_computation.36 | convolution fusion | flops 80813824 | bytes 6895233 | tf_op jit(solution)/shard_map/dot_general | solution.py:16
  135.2 1.2 copy-done.5
  136.5 1.4 fusion.17
  137.8 1.5 collective-permute-start.1
  139.3 2.1 %collective-permute-done.1 = bf16[128,1536]{1,0:T(8,128)(2,1)S(1)} collective-permute-done((bf16[128,1536]{1,0:T(8,128)(2,1)S(1)}, bf16[128,1536]{1,0:T(8,128)(2,1)S(1)}, u32[]{:S(2)}, u32[]{:S(2)}) %collective-permute-start.1) | collective-permute-done | bytes 393248 | tf_op jit(solution)/shard_map/ppermute | solution.py:307
  141.5 0.8 multiply_convert_fusion.2
  143.0 0.7 convolution_convert_fusion.1
  143.7 0.9 pad_maximum_fusion.1.g_ref
  144.6 54.0 %share.1 = bf16[8,64,4608]{2,1,0:T(8,128)(2,1)} custom-call(bf16[64,4608]{1,0:T(8,128)(2,1)} %pad_maximum_fusion.1.g_ref), custom_call_target="tpu_custom_call" | custom-call | tf_op jit(solution)/shard_map/share/pallas_call | solution.py:201
  198.6 3.5 %fusion.12 = (f32[64,1536]{1,0:T(8,128)S(1)}, f32[64,1536]{1,0:T(8,128)S(1)}, f32[64,1536]{1,0:T(8,128)S(1)}, f32[64,1536]{1,0:T(8,128)S(1)}, f32[64,1536]{1,0:T(8,128)S(1)}, /*index=5*/f32[64,1536]{1,0:T(8,128)S(1)}) fusion(pred[8]{0:T(512)(128)(4,1)S(1)} %get-tuple-element.39, bf16[8,64,4608]{2,1,0:T(8,128)(2,1)} %share.1, ...), kind=kLoop, calls=%fused_computation.27 | loop fusion | flops 9633792 | bytes 3932208 | tf_op jit(solution)/shard_map/reduce_sum | solution.py:329
  202.0 5.9 %fusion.5 = (f32[64,3072]{1,0:T(8,128)S(1)}, f32[64,3072]{1,0:T(8,128)S(1)}, f32[64,3072]{1,0:T(8,128)S(1)}, f32[64,3072]{1,0:T(8,128)S(1)}, f32[64,3072]{1,0:T(8,128)S(1)}, /*index=5*/f32[64,3072]{1,0:T(8,128)S(1)}) fusion(pred[8]{0:T(512)(128)(4,1)S(1)} %get-tuple-element.39, bf16[8,64,4608]{2,1,0:T(8,128)(2,1)} %share.1, ...), kind=kLoop, calls=%fused_computation.17 | loop fusion | flops 19267584 | bytes 7864368 | tf_op jit(solution)/shard_map/reduce_sum | solution.py:329
  208.4 1.2 copy-done.10
  209.8 2.2 %copy-done.9 = f32[6,64,3072]{2,1,0:T(8,128)} copy-done((f32[6,64,3072]{2,1,0:T(8,128)}, f32[6,64,3072]{2,1,0:T(8,128)S(1)}, u32[]{:S(2)}) %copy-start.9) | copy-done | bytes 4718616
  (49 shorter events, 3.0 us)
Async XLA Ops:
  0.6 4.0 %copy-start.6 = (bf16[1,6,64,3072]{3,2,1,0:T(8,128)(2,1)S(1)}, bf16[1,6,64,3072]{3,2,1,0:T(8,128)(2,1)}, u32[]{:S(2)}) copy-start(bf16[1,6,64,3072]{3,2,1,0:T(8,128)(2,1)} %param.16) | copy-start | bytes 7077892
  4.6 1.3 copy-start.7
  5.9 0.8 copy-start.11
  5.9 0.8 copy-start.12
  8.4 1.3 copy-start.1
  9.7 101.8 %copy-start.13 = (f32[1,50]{1,0:T(1,128)S(1)}, f32[1,50]{1,0:T(1,128)}, u32[]{:S(2)}) copy-start(f32[1,50]{1,0:T(1,128)} %param.15) | copy-start | bytes 604
  9.7 102.6 %copy-start.2 = (bf16[128,3072]{1,0:T(8,128)(2,1)S(1)}, bf16[128,3072]{1,0:T(8,128)(2,1)}, u32[]{:S(2)}) copy-start(bf16[128,3072]{1,0:T(8,128)(2,1)} %param.11) | copy-start | bytes 2359300
  9.7 102.6 %copy-start.8 = (f32[1,3072]{1,0:T(1,128)S(1)}, f32[1,3072]{1,0:T(1,128)}, u32[]{:S(2)}) copy-start(f32[1,3072]{1,0:T(1,128)} %param.14) | copy-start | bytes 36868
  111.6 3.8 %copy-start = (bf16[3072,1536]{1,0:T(8,128)(2,1)}, bf16[3072,1536]{1,0:T(8,128)(2,1)S(1)}, u32[]{:S(2)}) copy-start(bf16[3072,1536]{1,0:T(8,128)(2,1)S(1)} %get-tuple-element.4) | copy-start | bytes 28311556
  115.4 6.4 %copy-start.4 = (f32[128,3072]{1,0:T(8,128)S(1)}, f32[128,3072]{1,0:T(8,128)}, u32[]{:S(2)}) copy-start(f32[128,3072]{1,0:T(8,128)} %param.12) | copy-start | bytes 4718596
  119.1 11.5 %collective-permute-start = (bf16[128,1536]{1,0:T(8,128)(2,1)}, bf16[128,1536]{1,0:T(8,128)(2,1)}, u32[]{:S(2)}, u32[]{:S(2)}) collective-permute-start(bf16[128,1536]{1,0:T(8,128)(2,1)} %fusion.15), channel_id=1, source_target_pairs={{0,1},{2,3},{4,5},{6,7},{8,9},{10,11},{12,13},{14,15},{16,17},{18,... | collective-permute-start | bytes 1179656 | tf_op jit(solution)/shard_map/ppermute | solution.py:289
  121.8 8.7 %copy-start.3 = (bf16[128,3072]{1,0:T(8,128)(2,1)S(1)}, bf16[128,3072]{1,0:T(8,128)(2,1)}, u32[]{:S(2)}) copy-start(bf16[128,3072]{1,0:T(8,128)(2,1)} %param.11) | copy-start | bytes 2359300
  121.8 8.7 %slice-start = ((bf16[128,3072]{1,0:T(8,128)(2,1)}), bf16[128,1536]{1,0:T(8,128)(2,1)S(1)}, s32[]{:S(2)}) async-start(bf16[128,3072]{1,0:T(8,128)(2,1)} %param.11), calls=%async_computation | async-start | bytes 786432 | tf_op jit(solution)/shard_map/slice | solution.py:290
  135.0 1.4 copy-start.5
  137.8 3.6 %collective-permute-start.1 = (bf16[128,1536]{1,0:T(8,128)(2,1)S(1)}, bf16[128,1536]{1,0:T(8,128)(2,1)S(1)}, u32[]{:S(2)}, u32[]{:S(2)}) collective-permute-start(bf16[128,1536]{1,0:T(8,128)(2,1)S(1)} %fusion.17), channel_id=1, source_target_pairs={{1,0},{3,2},{5,4},{7,6},{9,8},{11,10},{13,12},{15,14},{17,16},{19,... | collective-permute-start | bytes 1179656 | tf_op jit(solution)/shard_map/ppermute | solution.py:307
  208.2 1.4 copy-start.10
  209.8 2.2 %copy-start.9 = (f32[6,64,3072]{2,1,0:T(8,128)}, f32[6,64,3072]{2,1,0:T(8,128)S(1)}, u32[]{:S(2)}) copy-start(f32[6,64,3072]{2,1,0:T(8,128)S(1)} %bitcast_dynamic-update-slice_fusion) | copy-start | bytes 14155780

commit v3 on v2

--- a/solution.py
+++ b/solution.py
@@ -161,45 +161,56 @@
     )(w, f)
 
 
-def share_kernel(n, g_ref, g_out, send, recv, local):
-    half = g_ref.shape[0] // 2
+def share_kernel(n, cuts, g_ref, g_out, send, recv, local):
+    piece = g_ref.shape[0] // (2 * cuts)
     me = lax.axis_index("dp")
     p = ring_spot(me, n)
     nexts = (ring_index(p + 1, n), ring_index(p - 1, n))
     greet({"dp": nexts[0]}, {"dp": nexts[1]})
 
-    def copy(way, step):
+    def rows(way, cut):
+        return pl.ds((way * cuts + cut) * piece, piece)
+
+    def copy(way, step, cut):
         owner = ring_index(p - step if way == 0 else p + step, n)
-        part = pl.ds(way * half, half)
+        part = rows(way, cut)
         target = g_out.at[owner, part]
         source = g_ref.at[part] if step == 0 else target
-        return remote(source, target, send.at[way, step], recv.at[way, step], dp=nexts[way])
-
-    def arrival(way, step):
+        return remote(
+            source, target, send.at[way, step, cut], recv.at[way, step, cut], dp=nexts[way]
+        )
+
+    def arrival(way, step, cut):
         owner = ring_index(p - 1 - step if way == 0 else p + 1 + step, n)
-        target = g_out.at[owner, pl.ds(way * half, half)]
-        return remote(target, target, send.at[way, step], recv.at[way, step], dp=nexts[way])
-
-    for way in range(2):
-        copy(way, 0).start()
+        target = g_out.at[owner, rows(way, cut)]
+        return remote(
+            target, target, send.at[way, step, cut], recv.at[way, step, cut], dp=nexts[way]
+        )
+
+    for cut in range(cuts):
+        for way in range(2):
+            copy(way, 0, cut).start()
     keep = pltpu.make_async_copy(g_ref, g_out.at[me], local.at[0])
     keep.start()
     for step in range(n - 1):
-        for way in range(2):
-            arrival(way, step).wait_recv()
-            if step < n - 2:
-                copy(way, step + 1).start()
+        for cut in range(cuts):
+            for way in range(2):
+                arrival(way, step, cut).wait_recv()
+                if step < n - 2:
+                    copy(way, step + 1, cut).start()
     for step in range(n - 1):
-        for way in range(2):
-            copy(way, step).wait_send()
+        for cut in range(cuts):
+            for way in range(2):
+                copy(way, step, cut).wait_send()
     keep.wait()
 
 
 def share(n, g):
     rank, cut = g.shape
-    pairs = [pltpu.SemaphoreType.DMA((2, n - 1))] * 2
+    cuts = 2
+    pairs = [pltpu.SemaphoreType.DMA((2, n - 1, cuts))] * 2
     return pl.pallas_call(
-        functools.partial(share_kernel, n),
+        functools.partial(share_kernel, n, cuts),
         out_shape=jax.ShapeDtypeStruct((n, rank, cut), g.dtype),
         in_specs=[pl.BlockSpec(memory_space=pl.ANY)],
         out_specs=pl.BlockSpec(memory_space=pl.ANY),
@@ -207,6 +218,42 @@
         compiler_params=pltpu.CompilerParams(collective_id=1, has_side_effects=True),
         name="share",
     )(g)
+
+
+def settle_kernel(slot_ref, first_ref, g_ref, down_ref, up_ref):
+    width = down_ref.shape[3]
+    slot = first_ref[0] + pl.program_id(0)
+    down_ref[...] = jnp.zeros_like(down_ref)
+    up_ref[...] = jnp.zeros_like(up_ref)
+    for block in range(g_ref.shape[0]):
+
+        @pl.when(slot_ref[block] == slot)
+        def _():
+            down_ref[0, 0] += g_ref[block, :, :width].astype(f32)
+            up_ref[0, 0] += g_ref[block, :, width:].astype(f32)
+
+
+def settle(slot_of, first_slot, shared, slot_local, width):
+    blocks, rank, cut = shared.shape
+
+    def out_block(columns):
+        return pl.BlockSpec((1, 1, rank, columns), lambda j, *_: (0, j, 0, 0))
+
+    return pl.pallas_call(
+        settle_kernel,
+        grid_spec=pltpu.PrefetchScalarGridSpec(
+            num_scalar_prefetch=2,
+            grid=(slot_local,),
+            in_specs=[pl.BlockSpec((blocks, rank, cut), lambda j, *_: (0, 0, 0))],
+            out_specs=[out_block(width), out_block(cut - width)],
+        ),
+        out_shape=[
+            jax.ShapeDtypeStruct((1, slot_local, rank, width), f32),
+            jax.ShapeDtypeStruct((1, slot_local, rank, cut - width), f32),
+        ],
+        compiler_params=pltpu.CompilerParams(vmem_limit_bytes=32 << 20),
+        name="settle",
+    )(slot_of, jnp.reshape(first_slot, (1,)), shared)
 
 
 def body(
@@ -251,6 +298,18 @@
             total = jnp.where(mine[j], factors[j][None], total)
         return total
 
+    chosen = block_steps[:, None] == jnp.arange(gate.shape[0], dtype=jnp.int32)[None, :]
+    scales = jnp.sum(jnp.where(chosen, gate[None, :], 0.0), axis=1)
+    row_scale = jnp.repeat(scales, rows)[:, None]
+    live = (jnp.arange(rows, dtype=jnp.int32)[None, :] < block_fill[:, None]).reshape(-1, 1)
+
+    head = jnp.where(live, out_grad[:, :out_width], 0.0)
+    delta = (row_scale * head).astype(bf16)
+    start_values = latents.astype(f32)
+    start_inverse = lax.rsqrt(jnp.mean(start_values * start_values, axis=1, keepdims=True) + epsilon)
+    start_normed = (start_values * start_inverse * gain[None, :]).astype(bf16)
+    start_normed, delta = lax.optimization_barrier((start_normed, delta))
+
     if ringed:
         sent = jnp.concatenate([spread(down_factors[0]), spread(up_factors[0])], axis=2)
         frozen, factors = fetch(lanes, frozen_weight[0], sent)
@@ -261,12 +320,6 @@
         down = lax.psum_scatter(spread(down_factors[0]), "dp", scatter_dimension=0, tiled=True)
         up = lax.psum_scatter(spread(up_factors[0]), "dp", scatter_dimension=0, tiled=True)
 
-    chosen = block_steps[:, None] == jnp.arange(gate.shape[0], dtype=jnp.int32)[None, :]
-    scales = jnp.sum(jnp.where(chosen, gate[None, :], 0.0), axis=1)
-    row_scale = jnp.repeat(scales, rows)[:, None]
-    live = (jnp.arange(rows, dtype=jnp.int32)[None, :] < block_fill[:, None]).reshape(-1, 1)
-    masked = jnp.where(live, out_grad, 0.0)
-
     def per_block(left, right, dims):
         left = left.reshape(blocks_dev, -1, left.shape[-1])
         return [dot(left[b], right[b], dims) for b in range(blocks_dev)]
@@ -284,14 +337,12 @@
         return (values[:, :out_width] + update).astype(bf16)
 
     pair = [(0, 1)]
-    values, inverse, normed, low = forward(latents)
-    window = layer_out(latents, values, normed, low)
+    low = jnp.concatenate(per_block(start_normed, down, ((1,), (1,)))).astype(bf16)
+    window = layer_out(latents, start_values, start_normed, low)
     window = lax.ppermute(window, "section", pair)
     x = jnp.where(is_first, latents, jnp.concatenate([window, latents[:, out_width:]], axis=1))
     values, inverse, normed, low = forward(x)
 
-    head = masked[:, :out_width]
-    delta = (row_scale * head).astype(bf16)
     low_grad = jnp.concatenate(per_block(delta, up, ((1,), (1,)))).astype(bf16)
     norm_grad = dot(delta, frozen, ((1,), (1,))) + jnp.concatenate(
         per_block(low_grad, down, ((1,), (0,)))
@@ -318,7 +369,7 @@
     grad_up = outer(low, delta).astype(bf16)
     if ringed:
         shared = share(lanes, jnp.concatenate([grad_down[0], grad_up[0]], axis=1))
-        all_down, all_up = shared[:, :, :width], shared[:, :, width:]
+        return settle(slot_of, first_slot, shared, slot_local, width)
     else:
         all_down = lax.all_gather(grad_down, "dp", axis=0, tiled=True)
         all_up = lax.all_gather(grad_up, "dp", axis=0, tiled=True)

time: 212 us -> 199 us (0.939)
  other arithmetic: 19.5 us -> 11 us
  matrix products: 21.2 us -> 18.5 us
    reduce_sum x3 -> x1, other arithmetic: 10.9 us -> 1.52 us  [body(): jnp.mean(start_values * start_values, axis=1, keepdims=True) + epsilon]
    dot_general x6, matrix products: 21.2 us -> 18.5 us  [dot(): lax.dot_general(left, right, (dims, ((), ())), preferred_element_type=f32)]
    convert_element_type x0 -> x2, other arithmetic: none -> 2.69 us  [the longest x1 2.43 us: body(): start_values = latents.astype(f32)]
    convert_element_type x2 -> x1, other arithmetic: 2.58 us -> 0.14 us  [forward(): values = x.astype(f32)]
    pallas_call x1 -> x2, Pallas kernels: 54 us -> 53.3 us  [the longest x1 49 us: share(): pl.pallas_call(functools.partial(share_kernel, n, cuts), out_shape=jax.Sh...]
    unnamed x38 -> x26, local copies, waits for them, and re-layouts: 7.22 us -> 6.67 us
where the time goes in v3:
time: 199 us
  Pallas kernels  155 us (78%)
  matrix products  18.5 us (9%)
  other arithmetic  11 us (6%)
  local copies, waits for them, and re-layouts  6.91 us (3%)
  starting transfers between devices  2.61 us (1%)
  between operations  2.33 us (1%)
  waiting for transfers between devices  2.32 us (1%)
    pallas_call x1, Pallas kernels, fetch(): pl.pallas_call(functools.partial(fetch_kernel, n), out_shape=(jax.ShapeDt...  102 us
    pallas_call x1, Pallas kernels, share(): pl.pallas_call(functools.partial(share_kernel, n, cuts), out_shape=jax.Sh...  49 us
    dot_general x6, matrix products, dot(): lax.dot_general(left, right, (dims, ((), ())), preferred_element_type=f32)  18.5 us
    unnamed x26, local copies, waits for them, and re-layouts  6.67 us
    pallas_call x1, Pallas kernels, settle(): pl.pallas_call(settle_kernel, grid_spec=pltpu.PrefetchScalarGridSpec(num_...  4.33 us
  transfers between devices with their start and end apart: 2, of which 1 were waited for; matrix products, arithmetic and copies ran while one was open for 4% of the time, Pallas kernels for 0%

profile of v3, /device:TPU:0, one launch (start us, length us, event | category | flops | bytes accessed | tf_op | source)
XLA Modules:
  0.0 198.8 jit_solution(10021945974785547560)
XLA Ops:
  0.6 1.5 multiply_reduce_fusion.2
  2.2 2.4 %convert_element_type.47 = f32[128,3072]{1,0:T(8,128)} convert(bf16[128,3072]{1,0:T(8,128)(2,1)} %param.11) | non-fusion elementwise | flops 393216 | bytes 2359296 | tf_op jit(solution)/shard_map/convert_element_type | solution.py:308
  4.8 1.1 copy-done.8
  8.4 0.8 multiply_convert_fusion.3
  9.3 1.0 select_select_fusion
  11.4 0.9 copy-done.2
  12.3 101.8 %fetch.1 = (bf16[3072,1536]{1,0:T(8,128)(2,1)S(1)}, bf16[64,4608]{1,0:T(8,128)(2,1)S(1)}) custom-call(bf16[384,1536]{1,0:T(8,128)(2,1)S(1)} %bitcast.39, bf16[8,64,4608]{2,1,0:T(8,128)(2,1)S(1)} %pad_maximum_fusion.f_ref), custom_call_target="tpu_custom_call" | custom-call | tf_op jit(solution)/shard_map/fetch/pallas_call | solution.py:140
  114.1 2.8 %fusion.21 = f32[128,1536]{1,0:T(8,128)} fusion(bf16[128,3072]{1,0:T(8,128)(2,1)S(1)} %multiply_convert_fusion.1, bf16[3072,1536]{1,0:T(8,128)(2,1)S(1)} %get-tuple-element.7), kind=kOutput, calls=%fused_computation.63 | convolution fusion | flops 1207959552 | bytes 11010048 | tf_op jit(solution)/shard_map/dot_general | solution.py:16
  116.9 1.1 copy-done
  117.9 2.7 %fusion.3 = bf16[128,1536]{1,0:T(8,128)(2,1)S(1)} fusion(f32[128,1536]{1,0:T(8,128)} %fusion.21, bf16[128,3072]{1,0:T(8,128)(2,1)S(1)} %multiply_convert_fusion.1, f32[128,3072]{1,0:T(8,128)} %convert_element_type.47, f32[]{:T(128)} %fusion.18, bf16[64,4608]{1,0:T(8,128)(2,1)S(1)} %get-tuple-element.8), kind=kOutput, calls=%fused_computation.8 | convolution fusion | flops 76292096 | bytes 3342340 | tf_op jit(solution)/shard_map/dot_general | solution.py:16
  120.7 1.3 collective-permute-start
  122.0 8.1 %fusion.22 = f32[128,3072]{1,0:T(8,128)} fusion(bf16[128,1536]{1,0:T(8,128)(2,1)S(1)} %multiply_convert_fusion.3, bf16[3072,1536]{1,0:T(8,128)(2,1)} %copy-done), kind=kOutput, calls=%fused_computation.64 | convolution fusion | flops 1207959552 | bytes 11403264 | tf_op jit(solution)/shard_map/dot_general | solution.py:16
  130.1 3.5 %multiply_reduce_fusion.1 = (f32[128]{0:T(128)S(1)}, f32[128]{0:T(128)S(1)}, bf16[128,3072]{1,0:T(8,128)(2,1)S(1)}, f32[128,3072]{1,0:T(8,128)}) fusion(bf16[128,3072]{1,0:T(8,128)(2,1)S(1)} %copy-done.4, bf16[128,1536]{1,0:T(8,128)(2,1)S(1)} %slice-done, bf16[128,1536]{1,0:T(8,128)(2,1)S(1)} %collective-permute-done, pred[]{:T(512)S(6)} %eq.100, ...), kind=kOutput, calls=%fused_computation.12 | convolution fusion | flops 80224000 | bytes 6501377 | tf_op jit(solution)/shard_map/dot_general | solution.py:16
  133.8 1.2 copy-done.6
  135.0 1.4 fusion.5
  136.4 1.3 collective-permute-start.1
  137.7 2.3 %collective-permute-done.1 = bf16[128,1536]{1,0:T(8,128)(2,1)S(1)} collective-permute-done((bf16[128,1536]{1,0:T(8,128)(2,1)S(1)}, bf16[128,1536]{1,0:T(8,128)(2,1)S(1)}, u32[]{:S(2)}, u32[]{:S(2)}) %collective-permute-start.1) | collective-permute-done | bytes 393248 | tf_op jit(solution)/shard_map/ppermute | solution.py:358
  140.0 0.8 multiply_convert_fusion.2
  140.8 0.7 convolution_convert_fusion
  141.5 0.8 convolution_convert_fusion.1
  142.3 0.9 pad_maximum_fusion.1.g_ref
  143.1 49.0 %share.1.g_ref = bf16[8,64,4608]{2,1,0:T(8,128)(2,1)} custom-call(bf16[64,4608]{1,0:T(8,128)(2,1)} %pad_maximum_fusion.1.g_ref), custom_call_target="tpu_custom_call" | custom-call | tf_op jit(solution)/shard_map/share/pallas_call | solution.py:212
  192.1 2.3 %copy-done.1 = bf16[8,64,4608]{2,1,0:T(8,128)(2,1)S(1)} copy-done((bf16[8,64,4608]{2,1,0:T(8,128)(2,1)S(1)}, bf16[8,64,4608]{2,1,0:T(8,128)(2,1)}, u32[]{:S(2)}) %copy-start.1) | copy-done | bytes 4718616
  194.5 4.3 %settle.1 = (f32[1,6,64,3072]{3,2,1,0:T(8,128)}, f32[1,6,64,1536]{3,2,1,0:T(8,128)}) custom-call(s32[8]{0:T(128)S(1)} %select_reduce_fusion.slot_ref, s32[1]{0:T(128)} %bitcast.first_ref, bf16[8,64,4608]{2,1,0:T(8,128)(2,1)S(1)} %copy-done.1), custom_call_target="tpu_custom_call" | custom-call | tf_op jit(solution)/shard_map/settle/pallas_call | solution.py:242
  (36 shorter events, 2.6 us)
Async XLA Ops:
  0.6 4.0 %copy-start.7 = (bf16[1,6,64,3072]{3,2,1,0:T(8,128)(2,1)S(1)}, bf16[1,6,64,3072]{3,2,1,0:T(8,128)(2,1)}, u32[]{:S(2)}) copy-start(bf16[1,6,64,3072]{3,2,1,0:T(8,128)(2,1)} %param.16) | copy-start | bytes 7077892
  4.6 1.3 copy-start.8
  4.6 2.9 %copy-start.10 = (f32[1,50]{1,0:T(1,128)S(1)}, f32[1,50]{1,0:T(1,128)}, u32[]{:S(2)}) copy-start(f32[1,50]{1,0:T(1,128)} %param.15) | copy-start | bytes 604
  5.9 2.2 %copy-start.3 = (bf16[128,3072]{1,0:T(8,128)(2,1)S(1)}, bf16[128,3072]{1,0:T(8,128)(2,1)}, u32[]{:S(2)}) copy-start(bf16[128,3072]{1,0:T(8,128)(2,1)} %param.11) | copy-start | bytes 2359300
  5.9 2.2 %copy-start.9 = (f32[1,3072]{1,0:T(1,128)S(1)}, f32[1,3072]{1,0:T(1,128)}, u32[]{:S(2)}) copy-start(f32[1,3072]{1,0:T(1,128)} %param.14) | copy-start | bytes 36868
  5.9 2.5 %copy-start.5 = (f32[128,3072]{1,0:T(8,128)S(1)}, f32[128,3072]{1,0:T(8,128)}, u32[]{:S(2)}) copy-start(f32[128,3072]{1,0:T(8,128)} %param.12) | copy-start | bytes 4718596
  6.0 3.2 %copy-start.11 = (s32[48]{0:T(128)S(1)}, s32[48]{0:T(128)}, u32[]{:S(2)}) copy-start(s32[48]{0:T(128)} %param.19) | copy-start | bytes 580
  6.0 3.2 %copy-start.12 = (s32[8]{0:T(128)S(1)}, s32[8]{0:T(128)}, u32[]{:S(2)}) copy-start(s32[8]{0:T(128)} %param.18) | copy-start | bytes 100
  11.0 1.3 copy-start.2
  114.1 3.9 %copy-start = (bf16[3072,1536]{1,0:T(8,128)(2,1)}, bf16[3072,1536]{1,0:T(8,128)(2,1)S(1)}, u32[]{:S(2)}) copy-start(bf16[3072,1536]{1,0:T(8,128)(2,1)S(1)} %get-tuple-element.7) | copy-start | bytes 28311556
  120.7 9.4 %collective-permute-start = (bf16[128,1536]{1,0:T(8,128)(2,1)S(1)}, bf16[128,1536]{1,0:T(8,128)(2,1)S(1)}, u32[]{:S(2)}, u32[]{:S(2)}) collective-permute-start(bf16[128,1536]{1,0:T(8,128)(2,1)S(1)} %fusion.3), channel_id=1, source_target_pairs={{0,1},{2,3},{4,5},{6,7},{8,9},{10,11},{12,13},{14,15},{16,17},{18,... | collective-permute-start | bytes 1179656 | tf_op jit(solution)/shard_map/ppermute | solution.py:342
  122.0 8.1 %copy-start.4 = (bf16[128,3072]{1,0:T(8,128)(2,1)S(1)}, bf16[128,3072]{1,0:T(8,128)(2,1)}, u32[]{:S(2)}) copy-start(bf16[128,3072]{1,0:T(8,128)(2,1)} %param.11) | copy-start | bytes 2359300
  122.0 8.1 %slice-start = ((bf16[128,3072]{1,0:T(8,128)(2,1)}), bf16[128,1536]{1,0:T(8,128)(2,1)S(1)}, s32[]{:S(2)}) async-start(bf16[128,3072]{1,0:T(8,128)(2,1)} %param.11), calls=%async_computation | async-start | bytes 786432 | tf_op jit(solution)/shard_map/slice | solution.py:343
  133.6 1.4 copy-start.6
  136.4 3.6 %collective-permute-start.1 = (bf16[128,1536]{1,0:T(8,128)(2,1)S(1)}, bf16[128,1536]{1,0:T(8,128)(2,1)S(1)}, u32[]{:S(2)}, u32[]{:S(2)}) collective-permute-start(bf16[128,1536]{1,0:T(8,128)(2,1)S(1)} %fusion.5), channel_id=1, source_target_pairs={{1,0},{3,2},{5,4},{7,6},{9,8},{11,10},{13,12},{15,14},{17,16},{19,... | collective-permute-start | bytes 1179656 | tf_op jit(solution)/shard_map/ppermute | solution.py:358
  192.1 2.3 %copy-start.1 = (bf16[8,64,4608]{2,1,0:T(8,128)(2,1)S(1)}, bf16[8,64,4608]{2,1,0:T(8,128)(2,1)}, u32[]{:S(2)}) copy-start(bf16[8,64,4608]{2,1,0:T(8,128)(2,1)} %share.1.g_ref) | copy-start | bytes 14155780
